TPU v7x, 1024 devices: a whole 8x8x8 slice. The times are simulated.
1024 devices in a mesh: node: 64 (over y, z), xnode: 16 (over x, core).
Axes of the slice: x: 8, y: 8, z: 8, core: 2. Of those that a mesh axis runs over, the one named last changes fastest.
Arguments:
- pooled: bfloat16 [3072, 65536], P('xnode', 'node'), may hold values from -6 to 6
- counts: int32 [3072, 256], P('xnode', 'node'), may hold values from 0 to 12, as said below
- dims: int32 [256], P('node'), may hold values from 128 to 512, as said below
- proj: bfloat16 [65536, 128], P('node'), may hold values from -0.375 to 0.375
- v_weight: bfloat16 [3, 32768, 256], P(None, 'node'), may hold values from -0.03125 to 0.03125
- u_weight: bfloat16 [3, 256, 32768], P(None, None, 'node'), may hold values from -0.375 to 0.375
- bias: float32 [3, 32768], P(None, 'node'), may hold values from -3 to 3
- cotangent: bfloat16 [3072, 32768], P('xnode', 'node'), may hold values from -6 to 6
Outputs:
- row_grads: bfloat16 [65536, 3072], P(('node', 'xnode'))
- proj_grad: float32 [65536, 128], P(('node', 'xnode'))
Inputs may be any that keep to these rules, and one draw needn't show every extreme that they name: counts of every feature have a largest value of their own between 4 and 12, reached in the first sample. `dims`: the widths of each aligned block of 4 features sum to 1024; each is 128, 256 or 512.
All inputs are finite; a program needn't handle non-finite values.
Results may differ from a plain program's by a relative error of at most 0.025.
Values may be sent and summed in bfloat16 or wider, within the bound.
A program may use at most 32 MiB of HBM per device.

v0:
```python
import jax
import jax.numpy as jnp
from jax import lax
from jax.sharding import PartitionSpec as P

LAYERS = 3


def on_device(pooled, counts, dims, proj, v_weight, u_weight, bias, cotangent):
    feat_here = dims.shape[0]
    packed = pooled.shape[1]
    proj_width = proj.shape[1]
    ends = jnp.cumsum(dims)
    starts = ends - dims
    column = lax.iota(jnp.int32, packed)
    one_hot = ((column[None, :] >= starts[:, None]) & (column[None, :] < ends[:, None])).astype(
        jnp.float32
    )
    widened = (one_hot.T[:, :, None].astype(jnp.bfloat16) * proj[:, None, :]).reshape(
        packed, feat_here * proj_width
    )
    live = (counts > 0).astype(jnp.float32)
    mask_wide = jnp.dot(live, one_hot, precision=lax.Precision.HIGHEST)
    masked = pooled * mask_wide.astype(jnp.bfloat16)
    start = jnp.dot(masked, widened, preferred_element_type=jnp.float32).astype(jnp.bfloat16)
    base = start.astype(jnp.float32)
    state = base
    outputs = []
    for layer in range(LAYERS):
        operand = state.astype(jnp.bfloat16)
        partial_low = jnp.dot(operand, v_weight[layer], preferred_element_type=jnp.float32)
        lowrank = lax.psum(partial_low, "node").astype(jnp.bfloat16)
        upward = jnp.dot(lowrank, u_weight[layer], preferred_element_type=jnp.float32) + bias[layer]
        outputs.append(upward)
        state = base * upward + state
    grad = cotangent.astype(jnp.float32)
    accum = jnp.zeros_like(grad)
    for layer in range(LAYERS - 1, -1, -1):
        accum = accum + grad * outputs[layer]
        dupward = (grad * base).astype(jnp.bfloat16)
        partial_back = lax.dot_general(
            dupward, u_weight[layer], (((1,), (1,)), ((), ())), preferred_element_type=jnp.float32
        )
        dlow = lax.psum(partial_back, "node").astype(jnp.bfloat16)
        grad = grad + lax.dot_general(
            dlow, v_weight[layer], (((1,), (1,)), ((), ())), preferred_element_type=jnp.float32
        )
    dstart = (accum + grad).astype(jnp.bfloat16)
    row_term = lax.dot_general(
        widened, dstart, (((1,), (1,)), ((), ())), preferred_element_type=jnp.float32
    )
    scale = live / jnp.maximum(counts.astype(jnp.float32), 1.0)
    scale_wide = jnp.dot(one_hot.T, scale.T, precision=lax.Precision.HIGHEST)
    row_local = (row_term * scale_wide).astype(jnp.bfloat16)
    row_grads = lax.all_to_all(row_local, "xnode", split_axis=0, concat_axis=1, tiled=True)
    piece_rows = packed // lax.axis_size("xnode")
    product = lax.dot_general(
        masked, dstart, (((0,), (0,)), ((), ())), preferred_element_type=jnp.float32
    )
    whole_term = jnp.sum(
        product.reshape(packed, feat_here, proj_width) * one_hot.T[:, :, None], axis=1
    )
    summed = lax.psum(whole_term.astype(jnp.bfloat16), "xnode").astype(jnp.float32)
    proj_grad = lax.dynamic_slice_in_dim(
        summed, lax.axis_index("xnode") * piece_rows, piece_rows, 0
    )
    return (row_grads, proj_grad)


def solution(mesh):
    in_specs = (
        P("xnode", "node"),
        P("xnode", "node"),
        P("node"),
        P("node", None),
        P(None, "node", None),
        P(None, None, "node"),
        P(None, "node"),
        P("xnode", "node"),
    )
    out_specs = (P(("node", "xnode"), None), P(("node", "xnode"), None))
    return jax.shard_map(
        on_device, mesh=mesh, in_specs=in_specs, out_specs=out_specs, check_vma=False
    )
```

profile of v0, /device:TPU:1, one launch (start us, length us, event | category | flops | bytes accessed | tf_op | source)
XLA Modules:
  0.0 1018.9 jit_solution(4606093817041309640)
XLA Ops:
  7.2 0.8 reduce-window.8
  8.0 0.7 bitcast_subtract_fusion
  8.6 0.1 fusion.60
  8.7 0.2 copy.17
  8.9 0.0 copy-start
  8.9 0.0 copy-start.1
  9.0 1.4 fusion.3
  10.4 5.9 broadcast_multiply_fusion
  16.3 0.4 convolution_convert_fusion.1
  16.6 0.0 copy-done
  16.7 0.0 copy-done.1
  16.7 0.0 copy-start.3
  16.7 0.2 fusion.17
  16.9 1.2 fusion.33
  18.1 241.2 %all-reduce.9 = (bf16[192,256]{1,0:T(8,128)(2,1)S(1)}, bf16[192,256]{1,0:T(8,128)(2,1)S(1)}) all-reduce(f32[192,256]{1,0:T(8,128)S(1)} %fusion.17, f32[192,256]{1,0:T(8,128)S(1)} %fusion.33), channel_id=1, replica_groups=mesh['node'=64,'xnode'=16] {'node'}, use_global_device_ids=true, to_apply=%region_4.5 | all-reduce | flops 98304 | bytes 589824 | tf_op jit(solution)/shard_map/psum | solution.py:44
  259.3 1.2 convolution_add_fusion.2
  260.5 0.9 fusion.23
  261.4 0.0 copy-done.3
  261.4 0.2 convolution_add_fusion.5
  261.6 1.2 fusion.27
  262.8 222.2 %all-reduce.10 = (bf16[192,256]{1,0:T(8,128)(2,1)S(1)}, bf16[192,256]{1,0:T(8,128)(2,1)S(1)}) all-reduce(f32[192,256]{1,0:T(8,128)} %fusion.23, f32[192,256]{1,0:T(8,128)S(1)} %fusion.27), channel_id=1, replica_groups=mesh['node'=64,'xnode'=16] {'node'}, use_global_device_ids=true, to_apply=%region_5.6 | all-reduce | flops 98304 | bytes 589824 | tf_op jit(solution)/shard_map/psum | solution.py:44
  485.0 1.2 convolution_add_fusion.1
  486.2 1.2 convolution_add_fusion.4
  487.4 1.9 fusion.21
  489.2 1.9 fusion.29
  491.1 224.2 %all-reduce.11 = (bf16[192,256]{1,0:T(8,128)(2,1)S(1)}, bf16[192,256]{1,0:T(8,128)(2,1)S(1)}) all-reduce(f32[192,256]{1,0:T(8,128)} %fusion.21, f32[192,256]{1,0:T(8,128)} %fusion.29), channel_id=1, replica_groups=mesh['node'=64,'xnode'=16] {'node'}, use_global_device_ids=true, to_apply=%region_3.4 | all-reduce | flops 98304 | bytes 589824 | tf_op jit(solution)/shard_map/psum | solution.py:32
  715.3 1.2 fusion.5
  716.4 0.0 copy-start.2
  716.5 1.2 fusion.6
  717.7 0.5 fusion.7
  718.2 0.0 copy-done.2
  718.2 0.6 fusion
  718.8 1.0 copy.18
  719.8 173.2 %all-to-all-start = ((bf16[16,64,192]{2,1,0:T(8,128)(2,1)}), bf16[16,64,192]{2,1,0:T(8,128)(2,1)S(1)}, u32[]{:S(2)}, u32[]{:S(2)}) async-start(bf16[16,64,192]{2,1,0:T(8,128)(2,1)} %bitcast.11), calls=%async_computation | async-start | bytes 1048576 | tf_op jit(solution)/shard_map/all_to_all | solution.py:55
  893.0 0.0 all-reduce.8.cloned.1.call-start
  893.0 0.5 fusion.74
  893.5 1.0 multiply_reduce_fusion
  894.5 0.0 all-reduce.8.cloned.1.call-update
  894.5 114.4 %all-reduce.8.cloned.1.call-done = bf16[1024,128]{0,1:T(8,128)(2,1)} async-done(((bf16[1024,128]{0,1:T(8,128)(2,1)}), bf16[1024,128]{0,1:T(8,128)(2,1)}) %all-reduce.8.cloned.1.call-update) | async-done | bytes 262160 | tf_op jit(solution)/shard_map/psum | solution.py:63
  1008.9 0.8 dynamic-slice_convert_fusion
  1009.7 0.7 copy.20
  1010.4 0.0 all-to-all-done
  1010.5 0.3 copy.19
  1010.7 1.3 all_to_all.17
  (1 shorter events, 0.0 us)
Async XLA Ops:
  8.9 7.7 copy-start
  8.9 7.7 copy-start.1
  16.7 244.7 %copy-start.3 = (f32[3,512]{1,0:T(4,128)S(1)}, f32[3,512]{1,0:T(4,128)}, u32[]{:S(2)}) copy-start(f32[3,512]{1,0:T(4,128)} %param.14) | copy-start | bytes 18436
  716.4 1.7 copy-start.2
  719.8 290.7 %all-to-all-start = ((bf16[16,64,192]{2,1,0:T(8,128)(2,1)}), bf16[16,64,192]{2,1,0:T(8,128)(2,1)S(1)}, u32[]{:S(2)}, u32[]{:S(2)}) async-start(bf16[16,64,192]{2,1,0:T(8,128)(2,1)} %bitcast.11), calls=%async_computation | async-start | bytes 1048576 | tf_op jit(solution)/shard_map/all_to_all | solution.py:55
  893.0 116.0 %all-reduce.8.cloned.1.call-start = ((), (), s32[]{:S(2)}) async-start(), calls=%async_computation.1 | async-start | bytes 524288 | tf_op jit(solution)/shard_map/psum | solution.py:63
Sparse Core Ops, SparseCore 0:
  896.7 112.1 all-reduce.7
where the time goes:
time: 1020 us
  blocking collectives  688 us (67%)
  starting transfers between devices  173 us (17%)
  waiting for transfers between devices  114 us (11%)
  matrix products  16.7 us (2%)
  between operations  14.2 us (1%)
    psum x2, blocking collectives, on_device(): dlow = lax.psum(partial_back, 'node').astype(jnp.bfloat16)  463 us
    psum x1, blocking collectives, on_device(): lowrank = lax.psum(partial_low, 'node').astype(jnp.bfloat16)  224 us
    all_to_all x1, starting transfers between devices, on_device(): lax.all_to_all(row_local, 'xnode', split_axis=0, concat_axis=1, tiled=True)  173 us
    psum x1, waiting for transfers between devices, on_device(): lax.psum(whole_term.astype(jnp.bfloat16), 'xnode').astype(jnp.float32)  114 us
  transfers between devices with their start and end apart: 2, of which 1 were waited for; matrix products, arithmetic and copies ran while one was open for 0% of the time, Pallas kernels for 0%

commit v1 on v0

v1 whole, which is shorter than its diff:
```python
import functools

import jax
import jax.numpy as jnp
from jax import lax
from jax.experimental import pallas as pl
from jax.experimental.pallas import tpu as pltpu
from jax.sharding import PartitionSpec as P

LAYERS = 3
SIDE = 8
CORES = 2
GROUPS = SIDE * CORES
SAMPLES = 192
RANK = 256
WIDTH = 512
FEATS = 4
E = 128
PACKED = 1024
PIECE = PACKED // GROUPS
SHARD = 48
F32 = jnp.float32
BF16 = jnp.bfloat16

NN = (((1,), (0,)), ((), ()))
NT = (((1,), (1,)), ((), ()))
TN = (((0,), (0,)), ((), ()))


def dot(a, b, dims=NN):
    return lax.dot_general(a, b, dims, preferred_element_type=F32)


def kernel(
    dims_ref, counts_ref, pooled_ref, proj_ref, v_ref, u_ref, bias_ref, cot_ref,
    row_ref, pg_ref,
    base, state, grads, ups, scale,
    send1, recv1, sum1, recv2, gath,
    wsend, wrecv, dsend, drecv, pgall,
    s1_sem, r1_sem, s2_sem, r2_sem, s3_sem, r3_sem,
    ws_sem, wr_sem, ds_sem, dr_sem, fs_sem, fr_sem,
):
    node = lax.axis_index("node")
    group = lax.axis_index("xnode")
    y, z = node // SIDE, node % SIDE
    x, core = group // CORES, group % CORES
    here = (y, z)

    def along(axis, to):
        return (to * SIDE + z, group) if axis == 0 else (y * SIDE + to, group)

    def copy(src, dst, ssem, rsem, device):
        return pltpu.make_async_remote_copy(
            src_ref=src, dst_ref=dst, send_sem=ssem, recv_sem=rsem,
            device_id=device, device_id_type=pl.DeviceIdType.MESH,
        )

    barrier = pltpu.get_barrier_semaphore()

    def greet(d, c):
        for axis in (0, 1):
            to = lax.rem(here[axis] + d, SIDE)
            pl.semaphore_signal(
                barrier, inc=1, device_id=along(axis, to), device_id_type=pl.DeviceIdType.MESH
            )
        return c

    def greet_x(d, c):
        to = lax.rem(group + d, GROUPS)
        pl.semaphore_signal(
            barrier, inc=1, device_id=(node, to), device_id_type=pl.DeviceIdType.MESH
        )
        return c

    lax.fori_loop(1, SIDE, greet, 0)
    lax.fori_loop(1, GROUPS, greet_x, 0)

    ends = []
    total = jnp.int32(0)
    for j in range(FEATS):
        total = total + dims_ref[j]
        ends.append(total)
    starts = [jnp.int32(0)] + ends[:-1]
    rows = lax.broadcasted_iota(jnp.int32, (PACKED, E), 0)
    proj32 = proj_ref[...].astype(F32)
    widened = jnp.concatenate(
        [
            jnp.where((rows >= starts[j]) & (rows < ends[j]), proj32, 0.0).astype(BF16)
            for j in range(FEATS)
        ],
        axis=1,
    )
    counts = counts_ref[...].astype(F32)
    wide = [jnp.broadcast_to(counts[:, j : j + 1], (SAMPLES, E)) for j in range(FEATS)]
    live = jnp.concatenate([jnp.where(w > 0, 1.0, 0.0) for w in wide], axis=1)
    scale[...] = live / jnp.concatenate([jnp.maximum(w, 1.0) for w in wide], axis=1)
    start = dot(pooled_ref[...], widened) * live
    base[...] = start.astype(BF16)
    state[...] = base[...].astype(F32)

    def pick(c, parts):
        out = parts[0]
        for j in range(1, FEATS):
            inside = jnp.full(parts[0].shape, c * E, jnp.int32) >= starts[j]
            out = jnp.where(inside, parts[j], out)
        return out

    pl.semaphore_wait(barrier, 2 * (SIDE - 1) + GROUPS - 1)

    def start1(r, k, partial):
        rounded = partial.astype(BF16)
        for i in range(SIDE):
            a, b = i % 4, i // 4
            send1[r, k, i] = rounded[a * SHARD : (a + 1) * SHARD, b * E : (b + 1) * E]

        def one(d, c):
            to = lax.rem(here[k] + d, SIDE)
            copy(
                send1.at[r, k, to], recv1.at[r, k, d - 1], s1_sem.at[r, k], r1_sem.at[r, k],
                along(k, to),
            ).start()
            return c

        lax.fori_loop(1, SIDE, one, 0)

    def settle(ref, sem):
        pltpu.make_async_copy(ref, ref, sem).wait()

    def start2(r, k):
        settle(recv1.at[r, k], r1_sem.at[r, k])
        acc = send1[r, k, here[k]].astype(F32)
        for d in range(SIDE - 1):
            acc = acc + recv1[r, k, d].astype(F32)
        sum1[r, k] = acc.astype(BF16)

        def one(d, c):
            to = lax.rem(here[1 - k] + d, SIDE)
            copy(
                sum1.at[r, k], recv2.at[r, k, d - 1], s2_sem.at[r, k], r2_sem.at[r, k],
                along(1 - k, to),
            ).start()
            return c

        lax.fori_loop(1, SIDE, one, 0)

    def start3(r, k):
        settle(recv2.at[r, k], r2_sem.at[r, k])
        acc = sum1[r, k].astype(F32)
        for d in range(SIDE - 1):
            acc = acc + recv2[r, k, d].astype(F32)
        gath[r, k, here[k]] = acc.astype(BF16)

        def one(d, c):
            to = lax.rem(here[k] + d, SIDE)
            mine = gath.at[r, k, here[k]]
            copy(mine, mine, s3_sem.at[r, k], r3_sem.at[r, k], along(k, to)).start()
            return c

        lax.fori_loop(1, SIDE, one, 0)

    def finish(r, k):
        settle(recv1.at[r, k], r3_sem.at[r, k])
        whole = gath[r, k]
        return jnp.concatenate(
            [whole[0:4].reshape(SAMPLES, E), whole[4:8].reshape(SAMPLES, E)], axis=1
        )

    def start_forward(r):
        start1(r, 0, dot(state[...].astype(BF16), v_ref[r]))

    def start_backward(r):
        product = (grads[r] * base[...].astype(F32)).astype(BF16)
        start1(r, 1, dot(product, u_ref[LAYERS - 1 - r], NT))

    start_forward(0)
    grads[0] = cot_ref[...].astype(F32)
    start_backward(0)

    for c in range(SIDE):
        cols = pooled_ref[:, c * E : (c + 1) * E].astype(F32)
        wsend[c] = (cols * pick(c, wide)).astype(BF16)

    def send_w(d, c):
        to = lax.rem(group + d, GROUPS)
        copy(wsend.at[to // CORES], wrecv.at[group], ws_sem, wr_sem, (node, to)).start()
        return c

    lax.fori_loop(1, GROUPS, send_w, 0)
    wrecv[group] = wsend[x]

    for r in range(LAYERS):
        start2(r, 0)
        start2(r, 1)
        start3(r, 0)
        start3(r, 1)
        up = dot(finish(r, 0), u_ref[r]) + bias_ref[r : r + 1, :]
        ups[r] = up
        if r < LAYERS - 1:
            state[...] = base[...].astype(F32) * up + state[...]
            start_forward(r + 1)
        grads[r + 1] = grads[r] + dot(finish(r, 1), v_ref[LAYERS - 1 - r], NT)
        if r < LAYERS - 1:
            start_backward(r + 1)

    acc = grads[0] * ups[2] + grads[1] * ups[1] + grads[2] * ups[0] + grads[3]
    scaled = acc * scale[...]
    parts = [scaled[:, j * E : (j + 1) * E] for j in range(FEATS)]
    for c in range(SIDE):
        dsend[c] = pick(c, parts).astype(BF16)

    def send_d(d, c):
        to = lax.rem(x + d, SIDE)
        copy(
            dsend.at[to], drecv.at[group], ds_sem, dr_sem.at[d - 1], (node, to * CORES + core)
        ).start()
        return c

    lax.fori_loop(1, SIDE, send_d, 0)
    sibling = (node, x * CORES + 1 - core)
    drecv[group] = dsend[x]
    copy(dsend.at[x], drecv.at[group], fs_sem, fr_sem, sibling).start()

    def forward_d(d, c):
        origin = lax.rem(x + SIDE - d, SIDE) * CORES + core
        block = drecv.at[origin]
        settle(block, dr_sem.at[d - 1])
        copy(block, block, fs_sem, fr_sem, sibling).start()
        return c

    lax.fori_loop(1, SIDE, forward_d, 0)
    settle(wrecv.at[0 : GROUPS - 1], wr_sem)
    settle(drecv.at[0:SIDE], fr_sem)
    every = drecv[...].reshape(GROUPS * SAMPLES, E)
    mine = proj_ref[pl.ds(pl.multiple_of(group * PIECE, PIECE), PIECE), :]
    row_ref[...] = dot(mine, every, NT).astype(BF16)
    pgall[...] = dot(wrecv[...].reshape(GROUPS * SAMPLES, E), every, TN)
    pg_ref[...] = pgall[pl.ds(pl.multiple_of(core * PIECE, PIECE), PIECE), :]

    for r in range(LAYERS):
        for k in range(2):
            settle(recv1.at[r, k], s1_sem.at[r, k])
            settle(recv1.at[r, k], s2_sem.at[r, k])
            settle(recv1.at[r, k], s3_sem.at[r, k])
    settle(wrecv.at[0 : GROUPS - 1], ws_sem)
    settle(drecv.at[0 : SIDE - 1], ds_sem)
    settle(drecv.at[0:SIDE], fs_sem)


def on_device(pooled, counts, dims, proj, v_weight, u_weight, bias, cotangent):
    vmem = pl.BlockSpec(memory_space=pltpu.VMEM)
    smem = pl.BlockSpec(memory_space=pltpu.SMEM)
    dma = pltpu.SemaphoreType.DMA
    pair = (LAYERS, 2)
    return pl.pallas_call(
        kernel,
        out_shape=(
            jax.ShapeDtypeStruct((PIECE, GROUPS * SAMPLES), BF16),
            jax.ShapeDtypeStruct((PIECE, E), F32),
        ),
        in_specs=[smem] + [vmem] * 7,
        out_specs=(vmem, vmem),
        scratch_shapes=[
            pltpu.VMEM((SAMPLES, WIDTH), BF16),
            pltpu.VMEM((SAMPLES, WIDTH), F32),
            pltpu.VMEM((LAYERS + 1, SAMPLES, WIDTH), F32),
            pltpu.VMEM((LAYERS, SAMPLES, WIDTH), F32),
            pltpu.VMEM((SAMPLES, WIDTH), F32),
            pltpu.VMEM(pair + (SIDE, SHARD, E), BF16),
            pltpu.VMEM(pair + (SIDE - 1, SHARD, E), BF16),
            pltpu.VMEM(pair + (SHARD, E), BF16),
            pltpu.VMEM(pair + (SIDE - 1, SHARD, E), BF16),
            pltpu.VMEM(pair + (SIDE, SHARD, E), BF16),
            pltpu.VMEM((SIDE, SAMPLES, E), BF16),
            pltpu.VMEM((GROUPS, SAMPLES, E), BF16),
            pltpu.VMEM((SIDE, SAMPLES, E), BF16),
            pltpu.VMEM((GROUPS, SAMPLES, E), BF16),
            pltpu.VMEM((E, E), F32),
            dma(pair), dma(pair), dma(pair), dma(pair), dma(pair), dma(pair),
            dma, dma, dma, dma((SIDE - 1,)), dma, dma,
        ],
        compiler_params=pltpu.CompilerParams(
            collective_id=0, has_side_effects=True, vmem_limit_bytes=40 * 1024 * 1024
        ),
        cost_estimate=pl.CostEstimate(
            flops=1_500_000_000, bytes_accessed=3_000_000, transcendentals=0
        ),
    )(dims, counts, pooled, proj, v_weight, u_weight, bias, cotangent)


def solution(mesh):
    in_specs = (
        P("xnode", "node"),
        P("xnode", "node"),
        P("node"),
        P("node", None),
        P(None, "node", None),
        P(None, None, "node"),
        P(None, "node"),
        P("xnode", "node"),
    )
    out_specs = (P(("node", "xnode"), None), P(("node", "xnode"), None))
    return jax.shard_map(
        on_device, mesh=mesh, in_specs=in_specs, out_specs=out_specs, check_vma=False
    )
```

time: 1020 us -> 93.5 us (0.09)
  blocking collectives: 688 us -> 0 us
  starting transfers between devices: 173 us -> 0 us
  waiting for transfers between devices: 114 us -> 0 us
  Pallas kernels: 0 us -> 85.2 us
  matrix products: 16.7 us -> 0 us
  between operations: 14.2 us -> 0.69 us
    psum x3 -> x0, blocking collectives: 688 us -> none  [the longest x2 463 us: on_device(): dlow = lax.psum(partial_back, 'node').astype(jnp.bfloat16)]
    all_to_all x1 -> x0, starting transfers between devices: 173 us -> none  [on_device(): lax.all_to_all(row_local, 'xnode', split_axis=0, concat_axis=1, tiled=True)]
    psum x1 -> x0, waiting for transfers between devices: 114 us -> none  [on_device(): lax.psum(whole_term.astype(jnp.bfloat16), 'xnode').astype(jnp.float32)]
    pallas_call x0 -> x1, Pallas kernels: none -> 85.2 us  [on_device(): pl.pallas_call(kernel, out_shape=(jax.ShapeDtypeStruct((PIECE, GROUPS * S...]
    dot_general x17 -> x0, matrix products: 16.7 us -> none  [the longest x3 4.19 us: on_device(): jnp.dot(operand, v_weight[layer], preferred_element_type=jnp.float32)]
  transfers between devices with their start and end apart: 2 -> 0, of which waited for: 1 -> 0; matrix products, arithmetic and copies ran while one was open for 0% -> 0% of each run, Pallas kernels for 0% -> 0%
where the time goes in v1:
time: 93.5 us; the launch traced here: 93.2 us
  Pallas kernels  85.2 us (91%)
  local copies, waits for them, and re-layouts  7.31 us (8%)
    pallas_call x1, Pallas kernels, on_device(): pl.pallas_call(kernel, out_shape=(jax.ShapeDtypeStruct((PIECE, GROUPS * S...  85.2 us
    unnamed x17, local copies, waits for them, and re-layouts  7.31 us

profile of v1, /device:TPU:1, one launch (start us, length us, event | category | flops | bytes accessed | tf_op | source)
XLA Modules:
  0.0 93.2 jit_solution(16106777756198835927)
XLA Ops:
  0.6 0.0 copy-start.5
  0.6 0.0 copy-start.6
  0.7 0.8 copy.10.counts_ref
  1.5 0.0 copy-done.5
  1.5 0.0 copy-done.6
  1.5 0.0 copy-start
  1.5 1.1 %copy-done = bf16[3,512,256]{2,1,0:T(8,128)(2,1)S(1)} copy-done((bf16[3,512,256]{2,1,0:T(8,128)(2,1)S(1)}, bf16[3,512,256]{2,1,0:T(8,128)(2,1)}, u32[]{:S(2)}) %copy-start) | copy-done | bytes 786456
  2.6 0.0 copy-start.1
  2.6 1.1 %copy-done.1 = bf16[3,256,512]{2,1,0:T(8,128)(2,1)S(1)} copy-done((bf16[3,256,512]{2,1,0:T(8,128)(2,1)S(1)}, bf16[3,256,512]{2,1,0:T(8,128)(2,1)}, u32[]{:S(2)}) %copy-start.1) | copy-done | bytes 786456
  3.8 0.0 copy-start.2
  3.8 1.0 %copy-done.2 = bf16[192,1024]{1,0:T(8,128)(2,1)S(1)} copy-done((bf16[192,1024]{1,0:T(8,128)(2,1)S(1)}, bf16[192,1024]{1,0:T(8,128)(2,1)}, u32[]{:S(2)}) %copy-start.2) | copy-done | bytes 393240
  4.8 0.0 copy-start.3
  4.8 0.9 %copy-done.3 = bf16[1024,128]{1,0:T(8,128)(2,1)S(1)} copy-done((bf16[1024,128]{1,0:T(8,128)(2,1)S(1)}, bf16[1024,128]{1,0:T(8,128)(2,1)}, u32[]{:S(2)}) %copy-start.3) | copy-done | bytes 262168
  5.7 0.0 copy-start.4
  5.7 0.9 copy-done.4
  6.6 85.2 %shard_map.95 = (bf16[64,3072]{1,0:T(8,128)(2,1)S(1)}, f32[64,128]{1,0:T(8,128)S(1)}) custom-call(s32[4]{0:T(128)S(1)} %copy-done.6, s32[192,4]{1,0:T(8,128)S(1)} %copy.10.counts_ref, bf16[192,1024]{1,0:T(8,128)(2,1)S(1)} %copy-done.2, bf16[1024,128]{1,0:T(8,128)(2,1)S(1)} %copy-done.3, bf16[3,512,256]{2,1,0:T(8,128)(2,1)S(1)} %copy-done, ...), custom_call_target="tpu_custom_call" | custom-call | flops 1500000000 | bytes 3000000 | tf_op jit(solution)/shard_map/pallas_call | solution.py:254
  91.8 0.7 copy.13
  92.6 0.6 copy.14
Async XLA Ops:
  0.6 0.8 copy-start.5
  0.6 0.8 copy-start.6
  1.5 1.1 %copy-start = (bf16[3,512,256]{2,1,0:T(8,128)(2,1)S(1)}, bf16[3,512,256]{2,1,0:T(8,128)(2,1)}, u32[]{:S(2)}) copy-start(bf16[3,512,256]{2,1,0:T(8,128)(2,1)} %v_ref.1) | copy-start | bytes 2359300
  2.6 1.1 %copy-start.1 = (bf16[3,256,512]{2,1,0:T(8,128)(2,1)S(1)}, bf16[3,256,512]{2,1,0:T(8,128)(2,1)}, u32[]{:S(2)}) copy-start(bf16[3,256,512]{2,1,0:T(8,128)(2,1)} %u_ref.1) | copy-start | bytes 2359300
  3.8 1.0 %copy-start.2 = (bf16[192,1024]{1,0:T(8,128)(2,1)S(1)}, bf16[192,1024]{1,0:T(8,128)(2,1)}, u32[]{:S(2)}) copy-start(bf16[192,1024]{1,0:T(8,128)(2,1)} %pooled_ref.1) | copy-start | bytes 1179652
  4.8 0.9 %copy-start.3 = (bf16[1024,128]{1,0:T(8,128)(2,1)S(1)}, bf16[1024,128]{1,0:T(8,128)(2,1)}, u32[]{:S(2)}) copy-start(bf16[1024,128]{1,0:T(8,128)(2,1)} %proj_ref.1) | copy-start | bytes 786436
  5.7 0.9 copy-start.4

commit v2 on v1

v2 whole, which is shorter than its diff:
```python
import functools

import jax
import jax.numpy as jnp
from jax import lax
from jax.experimental import pallas as pl
from jax.experimental.pallas import tpu as pltpu
from jax.sharding import PartitionSpec as P

LAYERS = 3
SIDE = 8
CORES = 2
GROUPS = SIDE * CORES
SAMPLES = 192
RANK = 256
WIDTH = 512
FEATS = 4
E = 128
PACKED = 1024
PIECE = PACKED // GROUPS
SHARD = 48
ORDER = (4, 3, 5, 2, 6, 1, 7)
F32 = jnp.float32
BF16 = jnp.bfloat16

NN = (((1,), (0,)), ((), ()))
NT = (((1,), (1,)), ((), ()))
TN = (((0,), (0,)), ((), ()))


def dot(a, b, dims=NN):
    return lax.dot_general(a, b, dims, preferred_element_type=F32)


def kernel(
    dims_hbm, counts_hbm, pooled_hbm, proj_hbm, v_hbm, u_hbm, bias_hbm, cot_hbm,
    row_ref, pg_ref,
    dims_ref, counts_ref, pooled_ref, proj_ref, v_ref, u_ref, bias_ref, cot_ref,
    base, state, grads, ups, scale, cots, pre,
    send1, recv1, sum1, recv2, gath,
    wsend, wrecv, wturn, dsend, drecv, pgown, pgin,
    in_sem, s1_sem, r1_sem, s2_sem, r2_sem, s3_sem, r3_sem,
    ws_sem, wr_sem, ds_sem, dr_sem, fs_sem, fr_sem, ps_sem, pr_sem,
):
    node = lax.axis_index("node")
    group = lax.axis_index("xnode")
    y, z = node // SIDE, node % SIDE
    x, core = group // CORES, group % CORES
    here = (y, z)

    def along(axis, to):
        return (to * SIDE + z, group) if axis == 0 else (y * SIDE + to, group)

    def copy(src, dst, ssem, rsem, device):
        return pltpu.make_async_remote_copy(
            src_ref=src, dst_ref=dst, send_sem=ssem, recv_sem=rsem,
            device_id=device, device_id_type=pl.DeviceIdType.MESH,
        )

    barrier = pltpu.get_barrier_semaphore()
    for d in ORDER:
        for axis in (0, 1):
            to = lax.rem(here[axis] + d, SIDE)
            pl.semaphore_signal(
                barrier, inc=1, device_id=along(axis, to), device_id_type=pl.DeviceIdType.MESH
            )

    def greet_x(d, c):
        to = lax.rem(group + d, GROUPS)
        pl.semaphore_signal(
            barrier, inc=1, device_id=(node, to), device_id_type=pl.DeviceIdType.MESH
        )
        return c

    lax.fori_loop(1, GROUPS, greet_x, 0)

    pairs = {
        "dims": (dims_hbm, dims_ref),
        "counts": (counts_hbm, counts_ref),
        "pooled": (pooled_hbm, pooled_ref),
        "proj": (proj_hbm, proj_ref),
        "v0": (v_hbm.at[0], v_ref.at[0]),
        "u2": (u_hbm.at[2], u_ref.at[2]),
        "cot": (cot_hbm, cot_ref),
        "u0": (u_hbm.at[0], u_ref.at[0]),
        "v2": (v_hbm.at[2], v_ref.at[2]),
        "bias": (bias_hbm, bias_ref),
        "v1": (v_hbm.at[1], v_ref.at[1]),
        "u1": (u_hbm.at[1], u_ref.at[1]),
    }
    loads = {
        name: pltpu.make_async_copy(src, dst, in_sem.at[i])
        for i, (name, (src, dst)) in enumerate(pairs.items())
    }
    for load in loads.values():
        load.start()

    loads["dims"].wait()
    ends = []
    total = jnp.int32(0)
    for j in range(FEATS):
        total = total + dims_ref[j]
        ends.append(total)
    starts = [jnp.int32(0)] + ends[:-1]

    def inside(c, j):
        spot = jnp.full((SAMPLES, E), c * E, jnp.int32)
        return (spot >= starts[j]) & (spot < ends[j])

    def pick(c, parts):
        spot = jnp.full((SAMPLES, E), c * E, jnp.int32)
        out = parts[0]
        for j in range(1, FEATS):
            out = jnp.where(spot >= starts[j], parts[j], out)
        return out

    loads["counts"].wait()
    counts = counts_ref[...].astype(F32).astype(BF16)
    lane = lax.broadcasted_iota(jnp.int32, (FEATS, WIDTH), 1)
    first = lax.broadcasted_iota(jnp.int32, (FEATS, WIDTH), 0) * E
    spread = jnp.where((lane >= first) & (lane < first + E), 1.0, 0.0).astype(BF16)
    scale[...] = dot(counts, spread, TN)
    loads["pooled"].wait()
    loads["proj"].wait()
    blocks = [
        dot(pooled_ref[:, c * E : (c + 1) * E], proj_ref[c * E : (c + 1) * E, :])
        for c in range(SIDE)
    ]
    for j in range(FEATS):
        own = slice(j * E, (j + 1) * E)
        start = jnp.zeros((SAMPLES, E), F32)
        for c in range(SIDE):
            start = start + jnp.where(inside(c, j), blocks[c], 0.0)
        start = jnp.where(scale[:, own] > 0, start, 0.0).astype(BF16)
        base[:, own] = start
        state[:, own] = start.astype(F32)

    def start1(r, k, partial):
        rounded = partial.astype(BF16)
        for i in range(SIDE):
            a, b = i % 4, i // 4
            send1[r, k, i] = rounded[a * SHARD : (a + 1) * SHARD, b * E : (b + 1) * E]
        if r == 0 and k == 0:
            pl.semaphore_wait(barrier, 2 * (SIDE - 1) + GROUPS - 1)
        for d in ORDER:
            to = lax.rem(here[k] + d, SIDE)
            copy(
                send1.at[r, k, to], recv1.at[r, k, d - 1], s1_sem.at[r, k], r1_sem.at[r, k],
                along(k, to),
            ).start()

    def settle(ref, sem):
        pltpu.make_async_copy(ref, ref, sem).wait()

    def start2(r, k):
        settle(recv1.at[r, k], r1_sem.at[r, k])
        acc = send1[r, k, here[k]].astype(F32)
        for d in range(SIDE - 1):
            acc = acc + recv1[r, k, d].astype(F32)
        sum1[r, k] = acc.astype(BF16)
        for d in ORDER:
            to = lax.rem(here[1 - k] + d, SIDE)
            copy(
                sum1.at[r, k], recv2.at[r, k, d - 1], s2_sem.at[r, k], r2_sem.at[r, k],
                along(1 - k, to),
            ).start()

    def start3(r, k):
        settle(recv2.at[r, k], r2_sem.at[r, k])
        acc = sum1[r, k].astype(F32)
        for d in range(SIDE - 1):
            acc = acc + recv2[r, k, d].astype(F32)
        mine = gath.at[r, k, here[k]]
        gath[r, k, here[k]] = acc.astype(BF16)
        for d in ORDER:
            to = lax.rem(here[k] + d, SIDE)
            copy(mine, mine, s3_sem.at[r, k], r3_sem.at[r, k], along(k, to)).start()

    def finish(r, k):
        settle(recv1.at[r, k], r3_sem.at[r, k])
        whole = gath[r, k]
        return jnp.concatenate(
            [whole[0:4].reshape(SAMPLES, E), whole[4:8].reshape(SAMPLES, E)], axis=1
        )

    def start_forward(r):
        start1(r, 0, dot(state[...].astype(BF16), v_ref[r]))

    def start_backward(r):
        product = (grads[r] * base[...].astype(F32)).astype(BF16)
        start1(r, 1, dot(product, u_ref[LAYERS - 1 - r], NT))

    def share_w():
        column = lax.broadcasted_iota(jnp.int32, (FEATS, PACKED), 1)
        row = lax.broadcasted_iota(jnp.int32, (FEATS, PACKED), 0)
        low = jnp.zeros((FEATS, PACKED), jnp.int32)
        high = low
        for j in range(FEATS):
            low = jnp.where(row == j, starts[j], low)
            high = jnp.where(row == j, ends[j], high)
        member = jnp.where((column >= low) & (column < high), 1.0, 0.0).astype(BF16)
        weight = dot(counts, member, TN)
        for c in range(SIDE):
            own = slice(c * E, (c + 1) * E)
            wsend[c] = (pooled_ref[:, own].astype(F32) * weight[:, own]).astype(BF16)
        for d in ORDER:
            to = lax.rem(x + d, SIDE)
            copy(
                wsend.at[to], wrecv.at[x], ws_sem, wr_sem, (node, to * CORES + core)
            ).start()
        wrecv[x] = wsend[x]

    loads["v0"].wait()
    start_forward(0)
    loads["cot"].wait()
    grads[0] = cot_ref[...].astype(F32)
    loads["u2"].wait()
    start_backward(0)

    wide = scale[...]
    scale[...] = jnp.where(wide > 0, 1.0, 0.0) / jnp.maximum(wide, 1.0)
    for name in ("u0", "v2", "bias", "v1", "u1"):
        loads[name].wait()

    for r in range(LAYERS):
        last = r == LAYERS - 1
        start2(r, 0)
        start2(r, 1)
        if r == 0:
            share_w()
        start3(r, 0)
        start3(r, 1)
        if r == 1:
            settle(wrecv.at[0 : SIDE - 1], wr_sem)
            for c in range(SIDE):
                wturn[c] = wrecv[c].T
        if last:
            cot = grads[0]
            pre[...] = scale[...] * (
                grads[1] * ups[1] + grads[2] * ups[0] + grads[2] + cot * bias_ref[2:3, :]
            )
            cots[...] = scale[...] * cot
        up = dot(finish(r, 0), u_ref[r])
        if last:
            pre[...] = pre[...] + cots[...] * up
        else:
            up = up + bias_ref[r : r + 1, :]
            ups[r] = up
            state[...] = base[...].astype(F32) * up + state[...]
            start_forward(r + 1)
        down = dot(finish(r, 1), v_ref[LAYERS - 1 - r], NT)
        if last:
            pre[...] = pre[...] + scale[...] * down
        else:
            grads[r + 1] = grads[r] + down
            start_backward(r + 1)

    parts = [pre[:, j * E : (j + 1) * E] for j in range(FEATS)]
    for c in range(SIDE):
        dsend[c] = pick(c, parts).astype(BF16)
    for d in ORDER:
        to = lax.rem(x + d, SIDE)
        copy(
            dsend.at[to], drecv.at[group], ds_sem, dr_sem.at[d], (node, to * CORES + core)
        ).start()
    sibling = (node, x * CORES + 1 - core)
    copy(dsend.at[x], drecv.at[group], fs_sem, fr_sem.at[0], sibling).start()
    drecv[group] = dsend[x]

    for r in range(LAYERS):
        for k in range(2):
            settle(recv1.at[r, k], s1_sem.at[r, k])
            settle(recv1.at[r, k], s2_sem.at[r, k])
            settle(recv1.at[r, k], s3_sem.at[r, k])
    settle(wrecv.at[0 : SIDE - 1], ws_sem)

    mine = proj_ref[pl.ds(pl.multiple_of(group * PIECE, PIECE), PIECE), :]
    half = pl.ds(pl.multiple_of(core * PIECE, PIECE), PIECE)
    other = pl.ds(pl.multiple_of((1 - core) * PIECE, PIECE), PIECE)

    def use(d):
        chip = lax.rem(x + SIDE - d, SIDE)
        settle(drecv.at[chip * CORES + 1 - core], fr_sem.at[d])
        pair = drecv[pl.ds(chip * CORES, CORES)].reshape(CORES * SAMPLES, E)
        at = pl.ds(pl.multiple_of(chip * (CORES * SAMPLES), CORES * SAMPLES), CORES * SAMPLES)
        row_ref[:, at] = dot(mine, pair, NT).astype(BF16)

    pgown[...] = dot(wturn[x], dsend[x])
    waiting = [0]
    for d in ORDER:
        chip = lax.rem(x + SIDE - d, SIDE)
        block = drecv.at[chip * CORES + core]
        settle(block, dr_sem.at[d])
        copy(block, block, fs_sem, fr_sem.at[d], sibling).start()
        pgown[...] = pgown[...] + dot(wturn[chip], block[...])
        waiting.append(d)
        if d == ORDER[-1]:
            parting = copy(pgown.at[other], pgin, ps_sem, pr_sem, sibling)
            parting.start()
        if len(waiting) > 2:
            use(waiting.pop(0))
    for d in waiting:
        use(d)
    parting.wait()
    pg_ref[...] = pgown[half, :] + pgin[...]
    settle(drecv.at[0 : SIDE - 1], ds_sem)
    settle(drecv.at[0:SIDE], fs_sem)


def store_kernel(row_ref, pg_ref, row_out, pg_out, sems):
    moves = [
        pltpu.make_async_copy(row_ref, row_out, sems.at[0]),
        pltpu.make_async_copy(pg_ref, pg_out, sems.at[1]),
    ]
    for move in moves:
        move.start()
    for move in moves:
        move.wait()


def store(row_grads, proj_grad):
    vmem = pl.BlockSpec(memory_space=pltpu.VMEM)
    hbm = pl.BlockSpec(memory_space=pl.ANY)
    return pl.pallas_call(
        store_kernel,
        out_shape=(
            pltpu.HBM(row_grads.shape, row_grads.dtype),
            pltpu.HBM(proj_grad.shape, proj_grad.dtype),
        ),
        in_specs=[vmem, vmem],
        out_specs=(hbm, hbm),
        scratch_shapes=[pltpu.SemaphoreType.DMA((2,))],
    )(row_grads, proj_grad)


def on_device(pooled, counts, dims, proj, v_weight, u_weight, bias, cotangent):
    vmem = pl.BlockSpec(memory_space=pltpu.VMEM)
    hbm = pl.BlockSpec(memory_space=pl.ANY)
    dma = pltpu.SemaphoreType.DMA
    pair = (LAYERS, 2)
    inputs = (dims, counts.T, pooled, proj, v_weight, u_weight, bias, cotangent)
    results = pl.pallas_call(
        kernel,
        out_shape=(
            jax.ShapeDtypeStruct((PIECE, GROUPS * SAMPLES), BF16),
            jax.ShapeDtypeStruct((PIECE, E), F32),
        ),
        in_specs=[hbm] * 8,
        out_specs=(vmem, vmem),
        scratch_shapes=[pltpu.SMEM(dims.shape, dims.dtype)]
        + [pltpu.VMEM(a.shape, a.dtype) for a in inputs[1:]]
        + [
            pltpu.VMEM((SAMPLES, WIDTH), BF16),
            pltpu.VMEM((SAMPLES, WIDTH), F32),
            pltpu.VMEM((LAYERS, SAMPLES, WIDTH), F32),
            pltpu.VMEM((LAYERS - 1, SAMPLES, WIDTH), F32),
            pltpu.VMEM((SAMPLES, WIDTH), F32),
            pltpu.VMEM((SAMPLES, WIDTH), F32),
            pltpu.VMEM((SAMPLES, WIDTH), F32),
            pltpu.VMEM(pair + (SIDE, SHARD, E), BF16),
            pltpu.VMEM(pair + (SIDE - 1, SHARD, E), BF16),
            pltpu.VMEM(pair + (SHARD, E), BF16),
            pltpu.VMEM(pair + (SIDE - 1, SHARD, E), BF16),
            pltpu.VMEM(pair + (SIDE, SHARD, E), BF16),
            pltpu.VMEM((SIDE, SAMPLES, E), BF16),
            pltpu.VMEM((SIDE, SAMPLES, E), BF16),
            pltpu.VMEM((SIDE, E, SAMPLES), BF16),
            pltpu.VMEM((SIDE, SAMPLES, E), BF16),
            pltpu.VMEM((GROUPS, SAMPLES, E), BF16),
            pltpu.VMEM((E, E), F32),
            pltpu.VMEM((PIECE, E), F32),
            dma((12,)),
            dma(pair), dma(pair), dma(pair), dma(pair), dma(pair), dma(pair),
            dma, dma, dma, dma((SIDE,)), dma, dma((SIDE,)), dma, dma,
        ],
        compiler_params=pltpu.CompilerParams(
            collective_id=0, has_side_effects=True, vmem_limit_bytes=32 * 1024 * 1024
        ),
        cost_estimate=pl.CostEstimate(
            flops=1_500_000_000, bytes_accessed=3_000_000, transcendentals=0
        ),
    )(*[pltpu.with_memory_space_constraint(a, pltpu.HBM) for a in inputs])
    return store(*results)


def solution(mesh):
    in_specs = (
        P("xnode", "node"),
        P("xnode", "node"),
        P("node"),
        P("node", None),
        P(None, "node", None),
        P(None, None, "node"),
        P(None, "node"),
        P("xnode", "node"),
    )
    out_specs = (P(("node", "xnode"), None), P(("node", "xnode"), None))
    return jax.shard_map(
        on_device, mesh=mesh, in_specs=in_specs, out_specs=out_specs, check_vma=False
    )
```

time: 93.5 us -> 84.8 us (0.907)
  local copies, waits for them, and re-layouts: 7.31 us -> 1.36 us
  Pallas kernels: 85.2 us -> 82.6 us
    unnamed x17 -> x4, local copies, waits for them, and re-layouts: 7.31 us -> 1.36 us
    pallas_call x1, Pallas kernels: 85.2 us -> 80.9 us  [on_device(): pl.pallas_call(kernel, out_shape=(jax.ShapeDtypeStruct((PIECE, GROUPS * S...]
    pallas_call x0 -> x1, Pallas kernels: none -> 1.76 us  [store(): pl.pallas_call(store_kernel, out_shape=(pltpu.HBM(row_grads.shape, row_gr...]
where the time goes in v2:
time: 84.8 us; the launch traced here: 84.6 us
  Pallas kernels  82.6 us (97%)
  local copies, waits for them, and re-layouts  1.36 us (2%)
    pallas_call x1, Pallas kernels, on_device(): pl.pallas_call(kernel, out_shape=(jax.ShapeDtypeStruct((PIECE, GROUPS * S...  80.9 us
    pallas_call x1, Pallas kernels, store(): pl.pallas_call(store_kernel, out_shape=(pltpu.HBM(row_grads.shape, row_gr...  1.76 us

profile of v2, /device:TPU:1, one launch (start us, length us, event | category | flops | bytes accessed | tf_op | source)
XLA Modules:
  0.0 84.6 jit_solution(13604743995437691603)
XLA Ops:
  0.6 80.9 %shard_map.95 = (bf16[64,3072]{1,0:T(8,128)(2,1)S(1)}, f32[64,128]{1,0:T(8,128)S(1)}) custom-call(s32[4]{0:T(128)} %dims_hbm.1, s32[4,192]{1,0:T(4,128)} %bitcast.1, bf16[192,1024]{1,0:T(8,128)(2,1)} %pooled_hbm.1, bf16[1024,128]{1,0:T(8,128)(2,1)} %proj_hbm.1, bf16[3,512,256]{2,1,0:T(8,128)(2,1)} %v_hbm.1, bf16[3,256,512]{2,1,0:T(8,128)(2,1)} %u_hbm.1, ...), custom_call_target="tpu_custom_call" | custom-call | flops 1500000000 | bytes 3000000 | tf_op jit(solution)/shard_map/pallas_call | solution.py:342
  81.5 0.0 copy-start
  81.5 0.7 copy-done
  82.3 0.0 copy-start.1
  82.3 0.6 copy-done.1
  82.9 1.8 %shard_map.96 = (bf16[64,3072]{1,0:T(8,128)(2,1)}, f32[64,128]{1,0:T(8,128)}) custom-call(bf16[64,3072]{1,0:T(8,128)(2,1)} %copy-done, f32[64,128]{1,0:T(8,128)} %copy-done.1), custom_call_target="tpu_custom_call" | custom-call | tf_op jit(solution)/shard_map/pallas_call | solution.py:324
Async XLA Ops:
  81.5 0.8 copy-start
  82.3 0.6 copy-start.1

commit v3 on v2

--- a/solution.py
+++ b/solution.py
@@ -104,8 +104,7 @@
     starts = [jnp.int32(0)] + ends[:-1]
 
     def inside(c, j):
-        spot = jnp.full((SAMPLES, E), c * E, jnp.int32)
-        return (spot >= starts[j]) & (spot < ends[j])
+        return jnp.where((starts[j] <= c * E) & (ends[j] > c * E), 1.0, 0.0)
 
     def pick(c, parts):
         spot = jnp.full((SAMPLES, E), c * E, jnp.int32)
@@ -130,7 +129,7 @@
         own = slice(j * E, (j + 1) * E)
         start = jnp.zeros((SAMPLES, E), F32)
         for c in range(SIDE):
-            start = start + jnp.where(inside(c, j), blocks[c], 0.0)
+            start = start + inside(c, j) * blocks[c]
         start = jnp.where(scale[:, own] > 0, start, 0.0).astype(BF16)
         base[:, own] = start
         state[:, own] = start.astype(F32)
@@ -319,18 +318,18 @@
 
 
 def store(row_grads, proj_grad):
-    vmem = pl.BlockSpec(memory_space=pltpu.VMEM)
-    hbm = pl.BlockSpec(memory_space=pl.ANY)
+    here = pl.BlockSpec(memory_space=pl.ANY)
     return pl.pallas_call(
         store_kernel,
         out_shape=(
             pltpu.HBM(row_grads.shape, row_grads.dtype),
             pltpu.HBM(proj_grad.shape, proj_grad.dtype),
         ),
-        in_specs=[vmem, vmem],
-        out_specs=(hbm, hbm),
+        in_specs=[here, here],
+        out_specs=(here, here),
         scratch_shapes=[pltpu.SemaphoreType.DMA((2,))],
-    )(row_grads, proj_grad)
+        compiler_params=pltpu.CompilerParams(vmem_limit_bytes=4 * 1024 * 1024),
+    )(*[pltpu.with_memory_space_constraint(a, pltpu.VMEM) for a in (row_grads, proj_grad)])
 
 
 def on_device(pooled, counts, dims, proj, v_weight, u_weight, bias, cotangent):

time: 84.8 us -> 80.9 us (0.954)
  Pallas kernels: 82.6 us -> 80 us
  local copies, waits for them, and re-layouts: 1.36 us -> 0 us
    pallas_call x1, Pallas kernels: 80.9 us -> 79.3 us  [on_device(): pl.pallas_call(kernel, out_shape=(jax.ShapeDtypeStruct((PIECE, GROUPS * S...]
    unnamed x4 -> x0, local copies, waits for them, and re-layouts: 1.36 us -> none
    pallas_call x1, Pallas kernels: 1.76 us -> 0.77 us  [store(): pl.pallas_call(store_kernel, out_shape=(pltpu.HBM(row_grads.shape, row_gr...]
where the time goes in v3:
time: 80.9 us; the launch traced here: 80.7 us
  Pallas kernels  80 us (99%)
    pallas_call x1, Pallas kernels, on_device(): pl.pallas_call(kernel, out_shape=(jax.ShapeDtypeStruct((PIECE, GROUPS * S...  79.3 us

profile of v3, /device:TPU:1, one launch (start us, length us, event | category | flops | bytes accessed | tf_op | source)
XLA Modules:
  0.0 80.7 jit_solution(2024813194798186572)
XLA Ops:
  0.6 79.3 %shard_map.95 = (bf16[64,3072]{1,0:T(8,128)(2,1)S(1)}, f32[64,128]{1,0:T(8,128)S(1)}) custom-call(s32[4]{0:T(128)} %dims_hbm.1, s32[4,192]{1,0:T(4,128)} %bitcast.1, bf16[192,1024]{1,0:T(8,128)(2,1)} %pooled_hbm.1, bf16[1024,128]{1,0:T(8,128)(2,1)} %proj_hbm.1, bf16[3,512,256]{2,1,0:T(8,128)(2,1)} %v_hbm.1, bf16[3,256,512]{2,1,0:T(8,128)(2,1)} %u_hbm.1, ...), custom_call_target="tpu_custom_call" | custom-call | flops 1500000000 | bytes 3000000 | tf_op jit(solution)/shard_map/pallas_call | solution.py:341
  79.9 0.8 shard_map.96

commit v4 on v3

--- a/solution.py
+++ b/solution.py
@@ -19,6 +19,7 @@
 PACKED = 1024
 PIECE = PACKED // GROUPS
 SHARD = 48
+XORDER = (4, 1, 7, 3, 5, 2, 6)
 ORDER = (4, 3, 5, 2, 6, 1, 7)
 F32 = jnp.float32
 BF16 = jnp.bfloat16
@@ -58,21 +59,18 @@
         )
 
     barrier = pltpu.get_barrier_semaphore()
+    sibling = (node, x * CORES + 1 - core)
+
+    def greet(device):
+        pl.semaphore_signal(
+            barrier, inc=1, device_id=device, device_id_type=pl.DeviceIdType.MESH
+        )
+
     for d in ORDER:
         for axis in (0, 1):
-            to = lax.rem(here[axis] + d, SIDE)
-            pl.semaphore_signal(
-                barrier, inc=1, device_id=along(axis, to), device_id_type=pl.DeviceIdType.MESH
-            )
-
-    def greet_x(d, c):
-        to = lax.rem(group + d, GROUPS)
-        pl.semaphore_signal(
-            barrier, inc=1, device_id=(node, to), device_id_type=pl.DeviceIdType.MESH
-        )
-        return c
-
-    lax.fori_loop(1, GROUPS, greet_x, 0)
+            greet(along(axis, lax.rem(here[axis] + d, SIDE)))
+        greet((node, lax.rem(x + d, SIDE) * CORES + core))
+    greet(sibling)
 
     pairs = {
         "dims": (dims_hbm, dims_ref),
@@ -140,7 +138,7 @@
             a, b = i % 4, i // 4
             send1[r, k, i] = rounded[a * SHARD : (a + 1) * SHARD, b * E : (b + 1) * E]
         if r == 0 and k == 0:
-            pl.semaphore_wait(barrier, 2 * (SIDE - 1) + GROUPS - 1)
+            pl.semaphore_wait(barrier, 3 * (SIDE - 1) + 1)
         for d in ORDER:
             to = lax.rem(here[k] + d, SIDE)
             copy(
@@ -257,12 +255,11 @@
     parts = [pre[:, j * E : (j + 1) * E] for j in range(FEATS)]
     for c in range(SIDE):
         dsend[c] = pick(c, parts).astype(BF16)
-    for d in ORDER:
+    for d in XORDER:
         to = lax.rem(x + d, SIDE)
         copy(
             dsend.at[to], drecv.at[group], ds_sem, dr_sem.at[d], (node, to * CORES + core)
         ).start()
-    sibling = (node, x * CORES + 1 - core)
     copy(dsend.at[x], drecv.at[group], fs_sem, fr_sem.at[0], sibling).start()
     drecv[group] = dsend[x]
 
@@ -286,17 +283,17 @@
 
     pgown[...] = dot(wturn[x], dsend[x])
     waiting = [0]
-    for d in ORDER:
+    for d in XORDER:
         chip = lax.rem(x + SIDE - d, SIDE)
         block = drecv.at[chip * CORES + core]
         settle(block, dr_sem.at[d])
         copy(block, block, fs_sem, fr_sem.at[d], sibling).start()
         pgown[...] = pgown[...] + dot(wturn[chip], block[...])
         waiting.append(d)
-        if d == ORDER[-1]:
+        if d == XORDER[-1]:
             parting = copy(pgown.at[other], pgin, ps_sem, pr_sem, sibling)
             parting.start()
-        if len(waiting) > 2:
+        if len(waiting) > 4:
             use(waiting.pop(0))
     for d in waiting:
         use(d)
@@ -307,10 +304,12 @@
 
 
 def store_kernel(row_ref, pg_ref, row_out, pg_out, sems):
-    moves = [
-        pltpu.make_async_copy(row_ref, row_out, sems.at[0]),
-        pltpu.make_async_copy(pg_ref, pg_out, sems.at[1]),
-    ]
+    moves = [pltpu.make_async_copy(pg_ref, pg_out, sems.at[0])]
+    for i in range(4):
+        rows = pl.ds(i * 16, 16)
+        moves.append(
+            pltpu.make_async_copy(row_ref.at[rows], row_out.at[rows], sems.at[i + 1])
+        )
     for move in moves:
         move.start()
     for move in moves:
@@ -327,7 +326,7 @@
         ),
         in_specs=[here, here],
         out_specs=(here, here),
-        scratch_shapes=[pltpu.SemaphoreType.DMA((2,))],
+        scratch_shapes=[pltpu.SemaphoreType.DMA((5,))],
         compiler_params=pltpu.CompilerParams(vmem_limit_bytes=4 * 1024 * 1024),
     )(*[pltpu.with_memory_space_constraint(a, pltpu.VMEM) for a in (row_grads, proj_grad)])
 

time: 80.9 us -> 80.9 us (level)
  no operation moved by 1% of the time
where the time goes in v4:
time: 80.9 us; the launch traced here: 80.7 us
  Pallas kernels  80.1 us (99%)
    pallas_call x1, Pallas kernels, on_device(): pl.pallas_call(kernel, out_shape=(jax.ShapeDtypeStruct((PIECE, GROUPS * S...  79.3 us

profile of v4, /device:TPU:1, one launch (start us, length us, event | category | flops | bytes accessed | tf_op | source)
XLA Modules:
  0.0 80.7 jit_solution(5555037339862538534)
XLA Ops:
  0.6 79.3 %shard_map.95 = (bf16[64,3072]{1,0:T(8,128)(2,1)S(1)}, f32[64,128]{1,0:T(8,128)S(1)}) custom-call(s32[4]{0:T(128)} %dims_hbm.1, s32[4,192]{1,0:T(4,128)} %bitcast.1, bf16[192,1024]{1,0:T(8,128)(2,1)} %pooled_hbm.1, bf16[1024,128]{1,0:T(8,128)(2,1)} %proj_hbm.1, bf16[3,512,256]{2,1,0:T(8,128)(2,1)} %v_hbm.1, bf16[3,256,512]{2,1,0:T(8,128)(2,1)} %u_hbm.1, ...), custom_call_target="tpu_custom_call" | custom-call | flops 1500000000 | bytes 3000000 | tf_op jit(solution)/shard_map/pallas_call | solution.py:340
  80.0 0.8 shard_map.96

commit v5 on v4

--- a/solution.py
+++ b/solution.py
@@ -246,15 +246,18 @@
             state[...] = base[...].astype(F32) * up + state[...]
             start_forward(r + 1)
         down = dot(finish(r, 1), v_ref[LAYERS - 1 - r], NT)
-        if last:
-            pre[...] = pre[...] + scale[...] * down
-        else:
+        if not last:
             grads[r + 1] = grads[r] + down
             start_backward(r + 1)
 
-    parts = [pre[:, j * E : (j + 1) * E] for j in range(FEATS)]
+    scaled = pre[...] + scale[...] * down
+    parts = [scaled[:, j * E : (j + 1) * E] for j in range(FEATS)]
+    parts = [part.astype(BF16) for part in parts]
     for c in range(SIDE):
-        dsend[c] = pick(c, parts).astype(BF16)
+        block = jnp.zeros((SAMPLES, E), BF16)
+        for j in range(FEATS):
+            block = block + inside(c, j).astype(BF16) * parts[j]
+        dsend[c] = block
     for d in XORDER:
         to = lax.rem(x + d, SIDE)
         copy(
@@ -293,7 +296,7 @@
         if d == XORDER[-1]:
             parting = copy(pgown.at[other], pgin, ps_sem, pr_sem, sibling)
             parting.start()
-        if len(waiting) > 4:
+        if len(waiting) > 5:
             use(waiting.pop(0))
     for d in waiting:
         use(d)
@@ -304,12 +307,10 @@
 
 
 def store_kernel(row_ref, pg_ref, row_out, pg_out, sems):
-    moves = [pltpu.make_async_copy(pg_ref, pg_out, sems.at[0])]
-    for i in range(4):
-        rows = pl.ds(i * 16, 16)
-        moves.append(
-            pltpu.make_async_copy(row_ref.at[rows], row_out.at[rows], sems.at[i + 1])
-        )
+    moves = [
+        pltpu.make_async_copy(row_ref, row_out, sems.at[0]),
+        pltpu.make_async_copy(pg_ref, pg_out, sems.at[1]),
+    ]
     for move in moves:
         move.start()
     for move in moves:
@@ -326,7 +327,7 @@
         ),
         in_specs=[here, here],
         out_specs=(here, here),
-        scratch_shapes=[pltpu.SemaphoreType.DMA((5,))],
+        scratch_shapes=[pltpu.SemaphoreType.DMA((2,))],
         compiler_params=pltpu.CompilerParams(vmem_limit_bytes=4 * 1024 * 1024),
     )(*[pltpu.with_memory_space_constraint(a, pltpu.VMEM) for a in (row_grads, proj_grad)])
 

time: 80.9 us -> 80.3 us (level)
  no operation moved by 1% of the time
where the time goes in v5:
time: 80.3 us; the launch traced here: 80.2 us
  Pallas kernels  79.5 us (99%)
    pallas_call x1, Pallas kernels, on_device(): pl.pallas_call(kernel, out_shape=(jax.ShapeDtypeStruct((PIECE, GROUPS * S...  78.8 us

profile of v5, /device:TPU:1, one launch (start us, length us, event | category | flops | bytes accessed | tf_op | source)
XLA Modules:
  0.0 80.2 jit_solution(4397786821102830011)
XLA Ops:
  0.6 78.8 %shard_map.95 = (bf16[64,3072]{1,0:T(8,128)(2,1)S(1)}, f32[64,128]{1,0:T(8,128)S(1)}) custom-call(s32[4]{0:T(128)} %dims_hbm.1, s32[4,192]{1,0:T(4,128)} %bitcast.1, bf16[192,1024]{1,0:T(8,128)(2,1)} %pooled_hbm.1, bf16[1024,128]{1,0:T(8,128)(2,1)} %proj_hbm.1, bf16[3,512,256]{2,1,0:T(8,128)(2,1)} %v_hbm.1, bf16[3,256,512]{2,1,0:T(8,128)(2,1)} %u_hbm.1, ...), custom_call_target="tpu_custom_call" | custom-call | flops 1500000000 | bytes 3000000 | tf_op jit(solution)/shard_map/pallas_call | solution.py:341
  79.4 0.8 shard_map.96
